TPU v7x, 256 devices: a whole 4x4x8 slice. The times are simulated.
256 devices in a mesh: dp: 16 (over x_hi, z), expert: 16 (over y, x_lo, core).
Axes of the slice: x: 4 (x_hi: 2, x_lo: 2; x = x_hi * 2 + x_lo), y: 4, z: 8, core: 2. Of those that a mesh axis runs over, the one named last changes fastest.
Arguments:
- tokens: bfloat16 [65536, 4096], P(('dp', 'expert')), may hold values from -6 to 6
- chosen: int32 [256, 16, 32], P(('dp', 'expert')), may hold values from 0 to 255, as said below
- gates: float32 [256, 16, 32], P(('dp', 'expert')), may hold values from 0.25 to 1
- w_gate: bfloat16 [16, 4096, 768], P('expert', 'dp'), may hold values from -0.09375 to 0.09375
- w_up: bfloat16 [16, 4096, 768], P('expert', 'dp'), may hold values from -0.09375 to 0.09375
- w_down: bfloat16 [16, 768, 4096], P('expert', None, 'dp'), may hold values from -0.21875 to 0.21875
Outputs:
- layer_out: bfloat16 [65536, 4096], P(('dp', 'expert'))
Inputs may be any that keep to these rules, and one draw needn't show every extreme that they name: `chosen`: for each slab and expert the 32 picked rows are distinct rows of the slab; every expert picks exactly 32 rows in every slab.
All inputs are finite; a program needn't handle non-finite values.
Results may differ from a plain program's by a relative error of at most 0.0049.
Values may be sent and summed in bfloat16 or wider, within the bound.
A program may use at most 128 MiB of HBM per device.

v0:
```python
import jax
import jax.numpy as jnp
from jax import lax
from jax.sharding import PartitionSpec as P


def shards(tokens, chosen, gates, w_gate, w_up, w_down):
    experts = chosen.shape[1]
    per_slab = chosen.shape[2]
    model_width = tokens.shape[1]
    pick_rows = chosen[0].reshape(-1)
    picked = jnp.take(tokens, pick_rows, axis=0).reshape(experts, per_slab, model_width)
    arrived = lax.all_to_all(picked, "expert", split_axis=0, concat_axis=0, tiled=True)
    inputs = arrived.reshape(-1, model_width)
    full_gate, full_up = (
        lax.all_gather(w_gate[0], "dp", axis=0, tiled=True),
        lax.all_gather(w_up[0], "dp", axis=0, tiled=True),
    )
    gate_part = jnp.dot(inputs, full_gate, preferred_element_type=jnp.float32)
    up_part = jnp.dot(inputs, full_up, preferred_element_type=jnp.float32)
    hidden = (jax.nn.silu(gate_part) * up_part).astype(jnp.bfloat16)
    expert_out = jnp.dot(
        hidden,
        lax.all_gather(w_down[0], "dp", axis=1, tiled=True),
        preferred_element_type=jnp.float32,
    )
    returned = lax.all_to_all(
        expert_out.reshape(experts, per_slab, model_width),
        "expert",
        split_axis=0,
        concat_axis=0,
        tiled=True,
    )
    weighted = gates[0][:, :, None] * returned
    combined = (
        jnp.zeros((tokens.shape[0], model_width), jnp.float32)
        .at[pick_rows]
        .add(weighted.reshape(-1, model_width))
    )
    return combined.astype(jnp.bfloat16)


def solution(mesh):
    in_specs = (
        P(("dp", "expert"), None),
        P(("dp", "expert"), None, None),
        P(("dp", "expert"), None, None),
        P("expert", "dp", None),
        P("expert", "dp", None),
        P("expert", None, "dp"),
    )
    out_specs = P(("dp", "expert"), None)
    return jax.shard_map(shards, mesh=mesh, in_specs=in_specs, out_specs=out_specs, check_vma=False)
```

profile of v0, /device:TPU:1, one launch (start us, length us, event | category | flops | bytes accessed | tf_op | source)
XLA Modules:
  0.0 526.5 jit_solution(6415197587071154605)
XLA Ops:
  6.5 0.0 copy-start
  6.5 0.0 all-gather.7.cloned.1.call-start
  6.5 0.7 all-gather.7.cloned.1.call-update
  7.3 0.0 all-gather.11.cloned.1.call-start
  7.3 0.7 all-gather.11.cloned.1.call-update
  8.0 0.0 all-gather.9.cloned.1.call-start
  8.1 0.7 all-gather.9.cloned.1.call-update
  8.7 0.8 reshape_squeeze.5
  9.5 0.0 copy-done
  9.5 0.0 copy-start.2
  9.6 4.4 gather_fusion
  14.0 0.0 copy-done.2
  14.0 2.6 broadcast_select_fusion
  16.6 63.2 %all_to_all.10 = bf16[16,32,4096]{2,1,0:T(8,128)(2,1)} all-to-all(bf16[16,32,4096]{2,1,0:T(8,128)(2,1)S(1)} %broadcast_select_fusion), channel_id=1, replica_groups=mesh['dp'=16,'expert'=16] {'expert'}, dimensions={0} | all-to-all | bytes 8388608 | tf_op jit(solution)/shard_map/all_to_all | solution.py:13
  79.8 59.4 %all-gather.7.cloned.1.call-done = bf16[1,4096,768]{2,1,0:T(8,128)(2,1)} async-done(((bf16[1,256,768]{2,1,0:T(8,128)(2,1)}), bf16[1,4096,768]{2,1,0:T(8,128)(2,1)}) %all-gather.7.cloned.1.call-update) | async-done | bytes 6291472 | tf_op jit(solution)/shard_map/all_gather | solution.py:16
  139.2 7.0 %fusion.4 = f32[512,768]{1,0:T(8,128)S(1)} fusion(bf16[512,4096]{1,0:T(8,128)(2,1)} %bitcast.28, bf16[1,4096,768]{2,1,0:T(8,128)(2,1)} %all-gather.7.cloned.1.call-done), kind=kOutput, calls=%fused_computation.6 | convolution fusion | flops 3221225472 | bytes 12058624 | tf_op jit(solution)/shard_map/dot_general | solution.py:19
  146.2 114.5 %all-gather.11.cloned.1.call-done = bf16[1,768,4096]{2,1,0:T(8,128)(2,1)} async-done(((bf16[1,768,256]{2,1,0:T(8,128)(2,1)}), bf16[1,768,4096]{2,1,0:T(8,128)(2,1)}) %all-gather.11.cloned.1.call-update) | async-done | bytes 6291472 | tf_op jit(solution)/shard_map/all_gather | solution.py:24
  260.7 117.1 %all-gather.9.cloned.1.call-done = bf16[1,4096,768]{2,1,0:T(8,128)(2,1)} async-done(((bf16[1,256,768]{2,1,0:T(8,128)(2,1)}), bf16[1,4096,768]{2,1,0:T(8,128)(2,1)}) %all-gather.9.cloned.1.call-update) | async-done | bytes 6291472 | tf_op jit(solution)/shard_map/all_gather | solution.py:17
  377.8 17.8 %fusion = f32[512,4096]{1,0:T(8,128)} fusion(bf16[1,768,4096]{2,1,0:T(8,128)(2,1)} %all-gather.11.cloned.1.call-done, f32[512,768]{1,0:T(8,128)S(1)} %fusion.4, bf16[512,4096]{1,0:T(8,128)(2,1)} %bitcast.29, bf16[1,4096,768]{2,1,0:T(8,128)(2,1)} %all-gather.9.cloned.1.call-done), kind=kOutput, calls=%fused_computation.2 | convolution fusion | flops 6444810240 | bytes 26738688 | tf_op jit(solution)/shard_map/dot_general | solution.py:22
  395.6 100.1 %all_to_all.11 = f32[16,32,4096]{2,1,0:T(8,128)S(1)} all-to-all(f32[16,32,4096]{2,1,0:T(8,128)} %bitcast.26), channel_id=1, replica_groups=mesh['dp'=16,'expert'=16] {'expert'}, dimensions={0} | all-to-all | bytes 16777216 | tf_op jit(solution)/shard_map/all_to_all | solution.py:27
  495.7 0.0 copy-done.3
  495.7 4.2 broadcast_multiply_fusion
  499.9 16.3 %scatter_custom_fusion = f32[256,4096]{1,0:T(8,128)} fusion(s32[512]{0:T(512)S(1)} %bitcast.32, f32[512,4096]{1,0:T(8,128)} %bitcast.27, f32[]{:T(128)} %constant.7.clone.1), kind=kCustom, calls=%fused_computation.10 | custom fusion | flops 2097152 | bytes 4194816 | tf_op jit(solution)/shard_map/scatter-add | solution.py:38
  516.2 3.8 convert_element_type.7
  (6 shorter events, 0.0 us)
Async XLA Ops:
  6.5 3.0 copy-start
  6.5 132.6 %all-gather.7.cloned.1.call-start = ((), (), s32[]{:S(2)}) async-start(), calls=%async_computation.2 | async-start | bytes 6684672 | tf_op jit(solution)/shard_map/all_gather | solution.py:16
  7.3 253.5 %all-gather.11.cloned.1.call-start = ((), (), s32[]{:S(2)}) async-start(), calls=%async_computation.4 | async-start | bytes 6684672 | tf_op jit(solution)/shard_map/all_gather | solution.py:24
  8.0 369.8 %all-gather.9.cloned.1.call-start = ((), (), s32[]{:S(2)}) async-start(), calls=%async_computation.3 | async-start | bytes 6684672 | tf_op jit(solution)/shard_map/all_gather | solution.py:17
  9.5 4.4 copy-start.2
  395.6 100.1 %copy-start.3 = (f32[1,16,32]{2,1,0:T(8,128)S(1)}, f32[1,16,32]{2,1,0:T(8,128)}, u32[]{:S(2)}) copy-start(f32[1,16,32]{2,1,0:T(8,128)} %param.8) | copy-start | bytes 6148
  499.9 20.1 %copy-start.1 = (bf16[256,4096]{1,0:T(8,128)(2,1)S(1)}, bf16[256,4096]{1,0:T(8,128)(2,1)}, u32[]{:S(2)}) copy-start(bf16[256,4096]{1,0:T(8,128)(2,1)} %param.6) | copy-start | bytes 6291460
Sparse Core Ops, SparseCore 0:
  9.9 129.1 all-gather.6
  141.6 119.0 all-gather.10
  263.3 114.4 all-gather.8
where the time goes:
time: 527 us
  waiting for transfers between devices  293 us (56%)
  blocking collectives  163 us (31%)
  other arithmetic  26.9 us (5%)
  matrix products  24.9 us (5%)
  between operations  13.1 us (2%)
    all_gather x1, waiting for transfers between devices, shards(): lax.all_gather(w_up[0], 'dp', axis=0, tiled=True)  117 us
    all_gather x1, waiting for transfers between devices, shards(): lax.all_gather(w_down[0], 'dp', axis=1, tiled=True)  115 us
    all_to_all x1, blocking collectives, shards(): lax.all_to_all(expert_out.reshape(experts, per_slab, model_width), 'exper...  100 us
    all_to_all x1, blocking collectives, shards(): lax.all_to_all(picked, 'expert', split_axis=0, concat_axis=0, tiled=True)  63.2 us
    all_gather x1, waiting for transfers between devices, shards(): lax.all_gather(w_gate[0], 'dp', axis=0, tiled=True)  59.4 us
    dot_general x1, matrix products, shards(): jnp.dot(hidden, lax.all_gather(w_down[0], 'dp', axis=1, tiled=True), pref...  17.8 us
    scatter-add x1, other arithmetic, shards(): combined = jnp.zeros((tokens.shape[0], model_width), jnp.float32).at[pick...  16.3 us
  transfers between devices with their start and end apart: 3, of which 3 were waited for; matrix products, arithmetic and copies ran while one was open for 3% of the time, Pallas kernels for 0%

commit v1 on v0

--- a/solution.py
+++ b/solution.py
@@ -21,7 +21,9 @@
     hidden = (jax.nn.silu(gate_part) * up_part).astype(jnp.bfloat16)
     expert_out = jnp.dot(
         hidden,
-        lax.all_gather(w_down[0], "dp", axis=1, tiled=True),
+        jnp.concatenate(
+            lax.all_to_all(jnp.stack([w_down[0]] * lax.axis_size("dp")), "dp", 0, 0), axis=1
+        ),
         preferred_element_type=jnp.float32,
     )
     returned = lax.all_to_all(

time: 527 us -> 490 us (0.930)
  blocking collectives: 163 us -> 99.7 us
  local copies, waits for them, and re-layouts: 5.2 us -> 28.1 us
  starting transfers between devices: 0.08 us -> 17.7 us
  waiting for transfers between devices: 293 us -> 281 us
    all_to_all x0 -> x2, waiting for transfers between devices: none -> 184 us  [the longest x1 154 us: shards(): lax.all_to_all(jnp.stack([w_down[0]] * lax.axis_size('dp')), 'dp', 0, 0)]
    all_gather x1 -> x0, waiting for transfers between devices: 115 us -> none  [shards(): lax.all_gather(w_down[0], 'dp', axis=1, tiled=True)]
    all_to_all x1 -> x0, blocking collectives: 63.2 us -> none  [shards(): lax.all_to_all(picked, 'expert', split_axis=0, concat_axis=0, tiled=True)]
    all_gather x1, waiting for transfers between devices: 59.4 us -> 0.01 us  [shards(): lax.all_gather(w_gate[0], 'dp', axis=0, tiled=True)]
    all_gather x1, waiting for transfers between devices: 117 us -> 95.7 us  [shards(): lax.all_gather(w_up[0], 'dp', axis=0, tiled=True)]
    reshape x0 -> x2, local copies, waits for them, and re-layouts: none -> 19.4 us  [shards(): jnp.concatenate(lax.all_to_all(jnp.stack([w_down[0]] * lax.axis_size('dp'...]
    all_to_all x0 -> x2, starting transfers between devices: none -> 17.7 us  [the longest x1 11.8 us: shards(): lax.all_to_all(jnp.stack([w_down[0]] * lax.axis_size('dp')), 'dp', 0, 0)]
    dot_general x1 -> x2, matrix products: 17.8 us -> 11.5 us  [the longest x1 8.05 us: shards(): up_part = jnp.dot(inputs, full_up, preferred_element_type=jnp.float32)]
  transfers between devices with their start and end apart: 3 -> 4, of which waited for: 3 -> 3; matrix products, arithmetic and copies ran while one was open for 3% -> 8% of each run, Pallas kernels for 0% -> 0%
where the time goes in v1:
time: 490 us; the launch traced here: 489 us
  waiting for transfers between devices  281 us (57%)
  blocking collectives  99.7 us (20%)
  other arithmetic  28.9 us (6%)
  local copies, waits for them, and re-layouts  28.1 us (6%)
  matrix products  20.1 us (4%)
  starting transfers between devices  17.7 us (4%)
  between operations  13.5 us (3%)
    all_to_all x1, waiting for transfers between devices, shards(): lax.all_to_all(jnp.stack([w_down[0]] * lax.axis_size('dp')), 'dp', 0, 0)  154 us
    all_to_all x1, blocking collectives, shards(): lax.all_to_all(expert_out.reshape(experts, per_slab, model_width), 'exper...  99.7 us
    all_gather x1, waiting for transfers between devices, shards(): lax.all_gather(w_up[0], 'dp', axis=0, tiled=True)  95.7 us
    all_to_all x1, waiting for transfers between devices, shards(): lax.all_to_all(picked, 'expert', split_axis=0, concat_axis=0, tiled=True)  30.3 us
    reshape x2, local copies, waits for them, and re-layouts, shards(): jnp.concatenate(lax.all_to_all(jnp.stack([w_down[0]] * lax.axis_size('dp'...  19.4 us
    scatter-add x1, other arithmetic, shards(): combined = jnp.zeros((tokens.shape[0], model_width), jnp.float32).at[pick...  16.3 us
    all_to_all x1, starting transfers between devices, shards(): lax.all_to_all(jnp.stack([w_down[0]] * lax.axis_size('dp')), 'dp', 0, 0)  11.8 us
  transfers between devices with their start and end apart: 4, of which 3 were waited for; matrix products, arithmetic and copies ran while one was open for 8% of the time, Pallas kernels for 0%

profile of v1, /device:TPU:1, one launch (start us, length us, event | category | flops | bytes accessed | tf_op | source)
XLA Modules:
  0.0 488.8 jit_solution(8849578220820727907)
XLA Ops:
  6.5 0.7 all-gather.5.cloned.1.call-update
  7.3 4.2 stack.3
  11.5 11.8 %all-to-all-start.1 = ((bf16[16,768,256]{2,1,0:T(8,128)(2,1)}), bf16[16,768,256]{2,1,0:T(8,128)(2,1)}, u32[]{:S(2)}, u32[]{:S(2)}) async-start(bf16[16,768,256]{2,1,0:T(8,128)(2,1)} %stack.3), calls=%async_computation.1 | async-start | bytes 12582912 | tf_op jit(solution)/shard_map/all_to_all | solution.py:25
  23.2 0.0 all-gather.7.cloned.1.call-start
  23.3 0.7 all-gather.7.cloned.1.call-update
  24.0 0.1 reshape_squeeze.5
  24.1 0.0 copy-done
  24.1 4.4 gather_fusion
  28.5 4.6 broadcast_select_fusion
  33.0 153.5 %all-to-all-done.1 = bf16[16,768,256]{2,1,0:T(8,128)(2,1)} async-done(((bf16[16,768,256]{2,1,0:T(8,128)(2,1)}), bf16[16,768,256]{2,1,0:T(8,128)(2,1)}, u32[]{:S(2)}, u32[]{:S(2)}) %all-to-all-start.1) | async-done | bytes 6291488 | tf_op jit(solution)/shard_map/all_to_all | solution.py:25
  186.5 5.9 %all-to-all-start = ((bf16[16,32,4096]{2,1,0:T(8,128)(2,1)}), bf16[16,32,4096]{2,1,0:T(8,128)(2,1)}, u32[]{:S(2)}, u32[]{:S(2)}) async-start(bf16[16,32,4096]{2,1,0:T(8,128)(2,1)} %broadcast_select_fusion), calls=%async_computation | async-start | bytes 8388608 | tf_op jit(solution)/shard_map/all_to_all | solution.py:13
  192.5 8.9 %copy.7 = bf16[768,16,256]{2,1,0:T(8,128)(2,1)} copy(bf16[768,16,256]{2,0,1:T(8,128)(2,1)} %bitcast.9) | data formatting | bytes 12582912 | tf_op jit(solution)/shard_map/reshape | solution.py:24
  201.4 10.5 %reshape.79 = bf16[768,4096,1]{1,0,2:T(8,128)(2,1)} reshape(bf16[768,16,256]{2,1,0:T(8,128)(2,1)} %copy.7) | data formatting | bytes 12582912 | tf_op jit(solution)/shard_map/reshape | solution.py:24
  211.9 30.3 %all-to-all-done = bf16[16,32,4096]{2,1,0:T(8,128)(2,1)} async-done(((bf16[16,32,4096]{2,1,0:T(8,128)(2,1)}), bf16[16,32,4096]{2,1,0:T(8,128)(2,1)}, u32[]{:S(2)}, u32[]{:S(2)}) %all-to-all-start) | async-done | bytes 4194336 | tf_op jit(solution)/shard_map/all_to_all | solution.py:13
  242.2 8.6 %fusion.2 = f32[512,768]{1,0:T(8,128)} fusion(bf16[512,4096]{1,0:T(8,128)(2,1)} %bitcast.4, bf16[1,4096,768]{2,1,0:T(8,128)(2,1)} %all-gather.5.cloned.1.call-done), kind=kOutput, calls=%fused_computation.4 | convolution fusion | flops 3221225472 | bytes 12058624 | tf_op jit(solution)/shard_map/dot_general | solution.py:19
  250.8 95.7 %all-gather.7.cloned.1.call-done = bf16[1,4096,768]{2,1,0:T(8,128)(2,1)} async-done(((bf16[1,256,768]{2,1,0:T(8,128)(2,1)}), bf16[1,4096,768]{2,1,0:T(8,128)(2,1)}) %all-gather.7.cloned.1.call-update) | async-done | bytes 6291472 | tf_op jit(solution)/shard_map/all_gather | solution.py:17
  346.5 8.1 %multiply_convert_fusion = bf16[512,768]{1,0:T(8,128)(2,1)S(1)} fusion(f32[512,768]{1,0:T(8,128)} %fusion.2, bf16[512,4096]{1,0:T(8,128)(2,1)} %bitcast.4, bf16[1,4096,768]{2,1,0:T(8,128)(2,1)} %all-gather.7.cloned.1.call-done), kind=kOutput, calls=%fused_computation.10 | convolution fusion | flops 3223584768 | bytes 12845056 | tf_op jit(solution)/shard_map/dot_general | solution.py:20
  354.5 3.4 fusion.8
  358.0 0.0 copy-start.4
  358.0 99.7 %all_to_all.15 = f32[16,32,4096]{2,1,0:T(8,128)S(1)} all-to-all(f32[16,32,4096]{2,1,0:T(8,128)S(1)} %fusion.8), channel_id=1, replica_groups=mesh['dp'=16,'expert'=16] {'expert'}, dimensions={0} | all-to-all | bytes 16777216 | tf_op jit(solution)/shard_map/all_to_all | solution.py:29
  457.7 0.0 copy-done.4
  457.7 4.2 broadcast_multiply_fusion
  461.9 16.3 %scatter_custom_fusion = f32[256,4096]{1,0:T(8,128)} fusion(s32[512]{0:T(512)S(1)} %bitcast.30, f32[512,4096]{1,0:T(8,128)} %bitcast.25, f32[]{:T(128)} %constant.7.clone.1), kind=kCustom, calls=%fused_computation.8 | custom fusion | flops 2097152 | bytes 4194816 | tf_op jit(solution)/shard_map/scatter-add | solution.py:40
  478.2 3.8 convert_element_type.7
  (12 shorter events, 0.0 us)
Async XLA Ops:
  6.5 17.5 %copy-start = (bf16[256,4096]{1,0:T(8,128)(2,1)S(1)}, bf16[256,4096]{1,0:T(8,128)(2,1)}, u32[]{:S(2)}) copy-start(bf16[256,4096]{1,0:T(8,128)(2,1)} %param.6) | copy-start | bytes 6291460
  6.5 235.6 %all-gather.5.cloned.1.call-start = ((), (), s32[]{:S(2)}) async-start(), calls=%async_computation.3 | async-start | bytes 6684672 | tf_op jit(solution)/shard_map/all_gather | solution.py:16
  11.4 12.5 %copy-start.3 = (s32[1,16,32]{2,1,0:T(8,128)S(1)}, s32[1,16,32]{2,1,0:T(8,128)}, u32[]{:S(2)}) copy-start(s32[1,16,32]{2,1,0:T(8,128)} %param.7) | copy-start | bytes 6148
  11.5 175.1 %all-to-all-start.1 = ((bf16[16,768,256]{2,1,0:T(8,128)(2,1)}), bf16[16,768,256]{2,1,0:T(8,128)(2,1)}, u32[]{:S(2)}, u32[]{:S(2)}) async-start(bf16[16,768,256]{2,1,0:T(8,128)(2,1)} %stack.3), calls=%async_computation.1 | async-start | bytes 12582912 | tf_op jit(solution)/shard_map/all_to_all | solution.py:25
  23.2 323.2 %all-gather.7.cloned.1.call-start = ((), (), s32[]{:S(2)}) async-start(), calls=%async_computation.4 | async-start | bytes 6684672 | tf_op jit(solution)/shard_map/all_gather | solution.py:17
  186.5 55.6 %all-to-all-start = ((bf16[16,32,4096]{2,1,0:T(8,128)(2,1)}), bf16[16,32,4096]{2,1,0:T(8,128)(2,1)}, u32[]{:S(2)}, u32[]{:S(2)}) async-start(bf16[16,32,4096]{2,1,0:T(8,128)(2,1)} %broadcast_select_fusion), calls=%async_computation | async-start | bytes 8388608 | tf_op jit(solution)/shard_map/all_to_all | solution.py:13
  346.4 8.1 %copy-start.2 = (bf16[768,4096,1]{1,0,2:T(8,128)(2,1)S(1)}, bf16[768,4096,1]{1,0,2:T(8,128)(2,1)}, u32[]{:S(2)}) copy-start(bf16[768,4096,1]{1,0,2:T(8,128)(2,1)} %reshape.79) | copy-start | bytes 18874372
  358.0 99.8 %copy-start.4 = (f32[1,16,32]{2,1,0:T(8,128)S(1)}, f32[1,16,32]{2,1,0:T(8,128)}, u32[]{:S(2)}) copy-start(f32[1,16,32]{2,1,0:T(8,128)} %param.8) | copy-start | bytes 6148
  461.9 20.1 %copy-start.1 = (bf16[256,4096]{1,0:T(8,128)(2,1)S(1)}, bf16[256,4096]{1,0:T(8,128)(2,1)}, u32[]{:S(2)}) copy-start(bf16[256,4096]{1,0:T(8,128)(2,1)} %param.6) | copy-start | bytes 6291460
Sparse Core Ops, SparseCore 0:
  9.9 219.7 all-gather.4
  232.3 114.0 all-gather.6
